TPU v7x, 256 devices: a whole 4x4x8 slice. The times are simulated.
256 devices in a mesh: pts: 32 (over z_lo, y, core), ctr: 8 (over x, z_hi).
Axes of the slice: x: 4, y: 4, z: 8 (z_hi: 2, z_lo: 4; z = z_hi * 4 + z_lo), core: 2. Of those that a mesh axis runs over, the one named last changes fastest.
Arguments:
- points: float32 [90, 65536], P(None, 'pts'), may hold values from -6 to 6
- centre_index: int32 [65536], P(('ctr', 'pts')), may hold values from 0 to 65535, as said below
- inv_scale: float32 [90], replicated, may hold values from 0.08 to 0.3
- left_cols: bfloat16 [64, 65536], P(None, 'pts'), may hold values from -0.375 to 0.375
- right_cols: bfloat16 [64, 65536], P(None, ('ctr', 'pts')), may hold values from -0.375 to 0.375
Outputs:
- point_side: float32 [64, 65536], P(None, 'pts')
- centre_side: float32 [64, 65536], P(None, ('ctr', 'pts'))
Inputs may be any that keep to these rules, and one draw needn't show every extreme that they name: `centre_index`: indices of the centres among the 65536 sampled points; repeats may occur, and both 0 and 65535 are taken in every draw.
All inputs are finite; a program needn't handle non-finite values.
Results may differ from a plain program's by a relative error of at most 0.012.
Values may be sent and summed in bfloat16 or wider, within the bound.
A program may use at most 64 MiB of HBM per device.

v0:
```python
import functools
import math

import jax
import jax.numpy as jnp
from jax import lax
from jax.experimental import pallas as pl
from jax.experimental.pallas import tpu as pltpu
from jax.sharding import PartitionSpec as P

F32, BF16, I32 = jnp.float32, jnp.bfloat16, jnp.int32
MESH = pl.DeviceIdType.MESH
LOG2E = math.log2(math.e)
FEAT = 90
ROWS = 96
COLS = 64
HERE = 2048
BLK = 256
CHIPS = 16
SLOTS = 48
PER = 8
TILE_I = 512
WIDE = 3
PART = HERE // 4
VMEM_LIMIT = 56 * 2**20


def pieces(value):
    first = value.astype(BF16).astype(F32)
    second = (value - first).astype(BF16).astype(F32)
    third = (value - first - second).astype(BF16).astype(F32)
    return first, second, third


def fused_kernel(
    rounds, pts_ref, inv_ref, idx_ref, left_ref, right_ref,
    point_ref, centre_ref, flag_ref,
    idx_all, rank_all, cols_s, cols_l, lookup, rows_out, rows_in,
    tables, lefts, blocks, rights, point_acc, own_part, to_home, at_home,
    pair_out, pair_in, x_out, x_in, z_out, z_in, back_out, back_in,
    flag_mine, flag_pair, flag_x, flag_z,
    idx_send, idx_recv, row_send, row_recv, right_send, right_recv,
    block_send, block_recv, home_send, home_recv, pair_send, pair_recv,
    x_send, x_recv, z_send, z_recv, back_send, back_recv, fx_send, fx_recv,
):
    me = lax.axis_index("pts")
    panel = lax.axis_index("ctr")
    chip, core = me // 2, lax.rem(me, 2)
    z, y = chip // 4, lax.rem(chip, 4)
    x, z_hi = panel // 2, lax.rem(panel, 2)
    pair = {"pts": chip * 2 + 1 - core}
    across = {"ctr": x * 2 + 1 - z_hi}

    def chip_at(m):
        return lax.rem(z + lax.rem(m, 4), 4) * 4 + lax.rem(y + m // 4, 4)

    def along_x(dx):
        return {"ctr": lax.rem(x + dx, 4) * 2 + z_hi}

    def remote(src, dst, send, recv, device):
        return pltpu.make_async_remote_copy(
            src_ref=src, dst_ref=dst, send_sem=send, recv_sem=recv,
            device_id=device, device_id_type=MESH,
        )

    def loop(first, last, act):
        def step(m, _):
            act(m)
            return 0

        lax.fori_loop(first, last, step, 0)

    barrier = pltpu.get_barrier_semaphore()
    pl.semaphore_signal(barrier, inc=1, device_id=across, device_id_type=MESH)
    for dx in (1, 2, 3):
        pl.semaphore_signal(barrier, inc=1, device_id=along_x(dx), device_id_type=MESH)
    loop(1, CHIPS, lambda m: pl.semaphore_signal(
        barrier, inc=1, device_id={"pts": chip_at(m) * 2 + core}, device_id_type=MESH
    ))
    pl.semaphore_signal(barrier, inc=1, device_id=pair, device_id_type=MESH)
    pl.semaphore_wait(barrier, CHIPS + 4)

    def rail(src, dst, send, recv, m):
        return remote(src, dst, send.at[m], recv, {"pts": chip_at(m) * 2 + core})

    def idx_copy(m):
        return rail(idx_ref, idx_all.at[chip], idx_send, idx_recv.at[chip], m)

    def idx_arrival(m):
        return rail(idx_ref, idx_all.at[chip_at(m)], idx_send, idx_recv.at[chip_at(m)], m)

    loop(1, CHIPS, lambda m: idx_copy(m).start())
    idx_all[chip] = idx_ref[...]

    class Spread:
        def __init__(self, held, send, recv):
            self.held, self.send, self.recv = held, send, recv

        def copy(self, m, source):
            there = chip_at(source)
            return rail(self.held.at[there], self.held.at[there], self.send, self.recv.at[there], m)

        def first(self):
            for d in (1, 2, 3):
                self.copy(4 * d, 0).start()
                self.copy(d, 0).start()

        def second(self):
            for dz in (1, 2, 3):
                self.arrive(dz)
                for dy in (1, 2, 3):
                    rail_on = {"pts": chip_at(4 * dy) * 2 + core}
                    there = chip_at(dz)
                    remote(
                        self.held.at[there], self.held.at[there],
                        self.send.at[dz + 4 * dy], self.recv.at[there], rail_on,
                    ).start()

        def arrive(self, m):
            self.copy(m, m).wait_recv()

        def drain(self, m):
            self.copy(m, 0).wait_send()

    right_spread = Spread(rights, right_send, right_recv)
    block_spread = Spread(blocks, block_send, block_recv)
    rights[chip] = right_ref[...]
    right_spread.first()

    eye = lax.broadcasted_iota(I32, (FEAT, FEAT), 0) == lax.broadcasted_iota(I32, (FEAT, FEAT), 1)
    scale = jnp.sum(jnp.where(eye, inv_ref[...], 0.0), axis=1, keepdims=True)
    scaled = (pts_ref[...] * scale).astype(BF16).astype(F32)
    half_norm = jnp.sum(scaled * scaled, axis=0, keepdims=True) * (-0.5 * LOG2E)
    ones = jnp.ones((3, HERE), F32)
    cols_s[ROWS:, :] = jnp.zeros((128 - ROWS, HERE), F32)
    cols_l[ROWS:, :] = jnp.zeros((128 - ROWS, HERE), F32)
    cols_s[0:FEAT, :] = scaled
    cols_l[0:FEAT, :] = scaled * LOG2E
    cols_s[FEAT:FEAT + 3, :] = ones
    cols_l[FEAT + 3:ROWS, :] = ones
    for place, piece in enumerate(pieces(half_norm)):
        cols_s[FEAT + 3 + place:FEAT + 4 + place, :] = piece
        cols_l[FEAT + place:FEAT + 1 + place, :] = piece
    for part in range(HERE // 128):
        span = slice(part * 128, (part + 1) * 128)
        high, low = part // 2, (part % 2) * 128
        lookup[core, low:low + 128, high * 128:(high + 1) * 128] = cols_s[:, span].T.astype(BF16)
    swap_lookup = remote(
        lookup.at[core], lookup.at[core], pair_send.at[0], pair_recv.at[0], pair
    )
    swap_lookup.start()
    for part in range(HERE // 128):
        span = slice(part * 128, (part + 1) * 128)
        turned = cols_l[:, span].T
        upper = turned.astype(BF16)
        tables[0, span, 0:128] = upper
        tables[0, span, 128:256] = (turned - upper.astype(F32)).astype(BF16)
    swap_table = remote(tables.at[0], tables.at[1], pair_send.at[1], pair_recv.at[1], pair)
    swap_table.start()
    swap_left = remote(left_ref, lefts.at[1], pair_send.at[2], pair_recv.at[2], pair)
    swap_left.start()
    lefts[0] = left_ref[...]

    earlier = (
        lax.broadcasted_iota(I32, (BLK, BLK), 0) < lax.broadcasted_iota(I32, (BLK, BLK), 1)
    ).astype(F32).astype(BF16)

    own_owner = idx_ref[...] >> 12
    own_hits = jnp.where(
        lax.broadcasted_iota(I32, (CHIPS, BLK), 0) == own_owner, 1.0, 0.0
    )
    own_rank = jnp.dot(own_hits.astype(BF16), earlier, preferred_element_type=F32)
    own_rank = jnp.sum(own_rank * own_hits, axis=0, keepdims=True).astype(I32)

    loop(1, CHIPS, lambda m: idx_arrival(m).wait_recv())

    owner = jnp.concatenate([idx_all[d] for d in range(CHIPS)], axis=0) >> 12
    hits = jnp.where(owner == chip, 1.0, 0.0)
    rank = jnp.dot(hits.astype(BF16), earlier, preferred_element_type=F32)
    rank = jnp.where(hits > 0.5, rank, -1.0)
    for d in range(CHIPS):
        rank_all[d] = rank[d:d + 1, :]

    slot_row = lax.broadcasted_iota(I32, (SLOTS, BLK), 0).astype(F32)
    low_col = lax.broadcasted_iota(I32, (SLOTS, BLK), 1)

    def row_copy(turn, m):
        return remote(
            rows_out.at[turn, m], rows_in.at[turn, chip],
            row_send.at[turn, m], row_recv.at[turn, chip], {"pts": chip_at(m) * 2 + core},
        )

    def row_arrival(turn, m):
        there = chip_at(m)
        return remote(
            rows_out.at[turn, m], rows_in.at[turn, there],
            row_send.at[turn, m], row_recv.at[turn, there], {"pts": there * 2 + core},
        )

    groups = CHIPS // PER

    def each_round(act):
        for turn in range(rounds):
            loop(1, CHIPS, functools.partial(act, turn))

    swap_lookup.wait_recv()

    def look_up(step):
        turn, number = step // groups, lax.rem(step, groups)
        first_slot = (turn * SLOTS).astype(F32)
        picks, highs = [], []
        for u in range(PER):
            home = chip_at(number * PER + u)
            local = (idx_all[home] & (2 * HERE - 1)).astype(F32)
            chosen = rank_all[home] - first_slot == slot_row
            key = jnp.sum(jnp.where(chosen, local + 1.0, 0.0), axis=1, keepdims=True)
            key = key.astype(I32) - 1
            highs.append(key >> 8)
            picks.append(jnp.where((key & 255) == low_col, 1.0, 0.0).astype(BF16))
        pick = jnp.concatenate(picks, axis=0)
        high = jnp.concatenate(highs, axis=0)
        rows = jnp.zeros((PER * SLOTS, 128), F32)
        for half in range(2):
            found = jnp.dot(pick, lookup[half], preferred_element_type=F32)
            for h in range(8):
                rows = jnp.where(high == half * 8 + h, found[:, h * 128:(h + 1) * 128], rows)
        rows = rows.astype(BF16)
        for u in range(PER):
            rows_out[turn, number * PER + u] = rows[u * SLOTS:(u + 1) * SLOTS, :]
        for u in range(PER):
            m = number * PER + u

            @pl.when(m > 0)
            def _():
                row_copy(turn, m).start()

    loop(0, rounds * groups, look_up)
    for turn in range(rounds):
        rows_in[turn, chip] = rows_out[turn, 0]

    right_spread.second()

    slot = lax.broadcasted_iota(I32, (CHIPS * SLOTS, BLK), 0)
    placed = []
    for turn in range(rounds):
        spot = own_rank - turn * SLOTS
        spot = jnp.where((spot >= 0) & (spot < SLOTS), own_owner * SLOTS + spot, -1)
        placed.append(jnp.where(slot == spot, 1.0, 0.0).astype(BF16))

    def count(source, most):
        here = jnp.sum(jnp.where(owner == source, 1.0, 0.0), axis=1, keepdims=True)
        return jnp.maximum(most, here)

    most = lax.fori_loop(0, CHIPS, count, jnp.zeros((CHIPS, 1), F32))
    flag_mine[0] = jnp.broadcast_to(jnp.max(most, axis=0, keepdims=True), (8, 128))
    point_acc[...] = jnp.zeros_like(point_acc)

    each_round(lambda turn, m: row_arrival(turn, m).wait_recv())
    centres = jnp.zeros((128, BLK), F32)
    for turn in range(rounds):
        centres = centres + lax.dot_general(
            rows_in[turn].reshape(CHIPS * SLOTS, 128), placed[turn],
            (((0,), (0,)), ((), ())), preferred_element_type=F32,
        )
    blocks[chip] = centres[0:ROWS, :].astype(BF16)

    block_spread.first()
    swap_table.wait_recv()
    swap_left.wait_recv()

    def home_copy(m):
        return rail(to_home.at[m], at_home.at[m], home_send, home_recv.at[m], m)

    def multiply(numbers):
        blank = jnp.zeros((128 - ROWS, BLK), BF16)
        sides, mates = [], []
        for m in numbers:
            there = chip_at(m)
            cut = blocks[there]
            sides.append(jnp.concatenate([cut, blank, cut, blank], axis=0))
            mates.append(rights[there])
        side = sides[0] if len(sides) == 1 else jnp.concatenate(sides, axis=1)
        mate = mates[0] if len(mates) == 1 else jnp.concatenate(mates, axis=1)
        total = None
        for own in range(2):
            for t in range(HERE // TILE_I):
                span = slice(t * TILE_I, (t + 1) * TILE_I)
                power = jnp.dot(tables[own, span, :], side, preferred_element_type=F32)
                kernel = jnp.exp2(jnp.minimum(power, 0.0)).astype(BF16)
                point_acc[own, :, span] += lax.dot_general(
                    mate, kernel, (((1,), (1,)), ((), ())), preferred_element_type=F32
                )
                part = jnp.dot(lefts[own, :, span], kernel, preferred_element_type=F32)
                total = part if total is None else total + part
        return total

    own_part[...] = multiply([0])
    block_spread.second()

    def advance(number):
        later = (number + 4) // 5
        numbers = [
            (1 - later) * (u + 1) + later * (number - 1 + 4 * (u + 1)) for u in range(WIDE)
        ]

        @pl.when(number > 0)
        def _():
            for m in numbers:
                right_spread.arrive(m)
                block_spread.arrive(m)

        total = multiply(numbers)
        for u, m in enumerate(numbers):
            to_home[m] = total[:, u * BLK:(u + 1) * BLK].astype(BF16)
            home_copy(m).start()

    loop(0, (CHIPS - 1) // WIDE, advance)

    pair_out[...] = point_acc[1].astype(BF16)
    swap_points = remote(pair_out, pair_in, pair_send.at[3], pair_recv.at[3], pair)
    swap_points.start()
    swap_flag = remote(flag_mine.at[0], flag_pair, pair_send.at[4], pair_recv.at[4], pair)
    swap_flag.start()

    def x_copy(dx):
        return remote(
            x_out.at[dx - 1], x_in.at[dx - 1], x_send.at[dx - 1], x_recv.at[dx - 1], along_x(dx)
        )

    def flag_x_copy(dx):
        return remote(
            flag_mine.at[1], flag_x.at[dx - 1], fx_send.at[dx - 1], fx_recv.at[dx - 1], along_x(dx)
        )

    def part_of(step):
        return pl.ds(pl.multiple_of(lax.rem(x + step, 4) * PART, PART), PART)

    swap_points.wait_recv()
    for dx in (1, 2, 3):
        span = part_of(dx)
        x_out[dx - 1] = (point_acc[0, :, span] + pair_in[:, span].astype(F32)).astype(BF16)
        x_copy(dx).start()
    swap_flag.wait_recv()
    flag_mine[1] = jnp.maximum(flag_mine[0], flag_pair[...])
    for dx in (1, 2, 3):
        flag_x_copy(dx).start()

    mine = part_of(0)
    total = point_acc[0, :, mine] + pair_in[:, mine].astype(F32)
    worst = flag_mine[1]
    for dx in (1, 2, 3):
        x_copy(dx).wait_recv()
        total = total + x_in[dx - 1].astype(F32)
    z_out[...] = total.astype(BF16)
    swap_z = remote(z_out, z_in, z_send.at[0], z_recv.at[0], across)
    swap_z.start()
    for dx in (1, 2, 3):
        flag_x_copy(dx).wait_recv()
        worst = jnp.maximum(worst, flag_x[dx - 1])
    flag_mine[2] = worst
    flag_across = remote(flag_mine.at[2], flag_z, z_send.at[1], z_recv.at[1], across)
    flag_across.start()

    loop(1, CHIPS, lambda m: home_copy(m).wait_recv())
    centre = own_part[...]
    for m in range(1, CHIPS):
        centre = centre + at_home[m].astype(F32)
    centre_ref[...] = centre

    swap_z.wait_recv()
    back_out[...] = (z_out[...].astype(F32) + z_in[...].astype(F32)).astype(BF16)

    def back_copy(dx):
        return remote(
            back_out, back_in.at[dx - 1], back_send.at[dx - 1], back_recv.at[dx - 1], along_x(dx)
        )

    for dx in (1, 2, 3):
        back_copy(dx).start()
    point_ref[:, mine] = back_out[...].astype(F32)
    flag_across.wait_recv()
    flag_ref[...] = jnp.maximum(flag_mine[2], flag_z[...])[0:1, 0:1]

    def drain(m):
        idx_copy(m).wait_send()
        right_spread.drain(m)
        block_spread.drain(m)
        home_copy(m).wait_send()

    loop(1, CHIPS, drain)
    each_round(lambda turn, m: row_copy(turn, m).wait_send())
    for copy in (swap_lookup, swap_table, swap_left, swap_points, swap_flag, swap_z, flag_across):
        copy.wait_send()
    for dx in (1, 2, 3):
        x_copy(dx).wait_send()
        flag_x_copy(dx).wait_send()

    for dx in (1, 2, 3):
        back_copy(dx).wait_recv()
        point_ref[:, part_of(4 - dx)] = back_in[dx - 1].astype(F32)
    for dx in (1, 2, 3):
        back_copy(dx).wait_send()


def fused(rounds, points, centre_index, inv_scale, left_cols, right_cols):
    vmem = pl.BlockSpec(memory_space=pltpu.VMEM)
    dma = pltpu.SemaphoreType.DMA
    buf = pltpu.VMEM
    return pl.pallas_call(
        functools.partial(fused_kernel, rounds),
        out_shape=(
            jax.ShapeDtypeStruct((COLS, HERE), F32),
            jax.ShapeDtypeStruct((COLS, BLK), F32),
            jax.ShapeDtypeStruct((1, 1), F32),
        ),
        in_specs=[vmem] * 5,
        out_specs=[vmem] * 3,
        scratch_shapes=[
            buf((CHIPS, 1, BLK), I32),
            buf((CHIPS, 1, BLK), F32),
            buf((128, HERE), F32),
            buf((128, HERE), F32),
            buf((2, 256, 1024), BF16),
            buf((rounds, CHIPS, SLOTS, 128), BF16),
            buf((rounds, CHIPS, SLOTS, 128), BF16),
            buf((2, HERE, 256), BF16),
            buf((2, COLS, HERE), BF16),
            buf((CHIPS, ROWS, BLK), BF16),
            buf((CHIPS, COLS, BLK), BF16),
            buf((2, COLS, HERE), F32),
            buf((COLS, BLK), F32),
            buf((CHIPS, COLS, BLK), BF16),
            buf((CHIPS, COLS, BLK), BF16),
            buf((COLS, HERE), BF16),
            buf((COLS, HERE), BF16),
            buf((3, COLS, PART), BF16),
            buf((3, COLS, PART), BF16),
            buf((COLS, PART), BF16),
            buf((COLS, PART), BF16),
            buf((COLS, PART), BF16),
            buf((3, COLS, PART), BF16),
            buf((3, 8, 128), F32),
            buf((8, 128), F32),
            buf((3, 8, 128), F32),
            buf((8, 128), F32),
        ]
        + [dma((CHIPS,))] * 2
        + [dma((rounds, CHIPS))] * 2
        + [dma((CHIPS,))] * 6
        + [dma((5,)), dma((5,)), dma((3,)), dma((3,)), dma((2,)), dma((2,))]
        + [dma((3,))] * 4,
        compiler_params=pltpu.CompilerParams(
            collective_id=rounds, has_side_effects=True, vmem_limit_bytes=VMEM_LIMIT
        ),
        name=f"nystrom_products_{rounds}",
    )(points, inv_scale[None, :], centre_index[None, :], left_cols, right_cols)


ROUNDS = -(-BLK // SLOTS)


def body(*arguments):
    point_side, centre_side, most = fused(1, *arguments)
    return lax.cond(
        most[0, 0] > SLOTS, lambda: fused(ROUNDS, *arguments)[:2], lambda: (point_side, centre_side)
    )


def solution(mesh):
    return jax.shard_map(
        body,
        mesh=mesh,
        in_specs=(P(None, "pts"), P(("ctr", "pts")), P(), P(None, "pts"), P(None, ("ctr", "pts"))),
        out_specs=(P(None, "pts"), P(None, ("ctr", "pts"))),
        check_vma=False,
    )
```

profile of v0, /device:TPU:4, one launch (start us, length us, event | category | flops | bytes accessed | tf_op | source)
XLA Modules:
  0.0 72.0 jit_solution(16325110352334192809)
XLA Ops:
  0.6 0.0 copy-start
  0.6 0.0 copy-start.1
  0.6 0.0 copy-start.2
  0.7 68.6 %nystrom_products_1.1 = (f32[64,2048]{1,0:T(8,128)S(1)}, f32[64,256]{1,0:T(8,128)S(1)}, f32[1,1]{1,0:T(1,128)}) custom-call(f32[90,2048]{1,0:T(8,128)} %pts_ref.1, f32[1,90]{1,0:T(1,128)} %bitcast.7, s32[1,256]{1,0:T(1,128)} %bitcast.5, bf16[64,2048]{1,0:T(8,128)(2,1)} %left_ref.1, bf16[64,256]{1,0:T(8,128)(2,1)} %right_ref.1), custom_call_target="tpu_custom_call" | custom-call | tf_op jit(solution)/shard_map/nystrom_products_1/pallas_call | solution.py:409
  69.9 0.0 copy-start.3
  69.9 0.0 copy-start.4
  69.9 0.0 copy-done
  69.9 0.0 copy-done.1
  69.9 0.0 copy-done.2
  69.9 0.6 copy-done.3
  70.6 0.0 copy-done.4
  70.6 0.8 %copy.17 = f32[64,2048]{1,0:T(8,128)} copy(f32[64,2048]{1,0:T(8,128)S(1)} %get-tuple-element.39) | data formatting | bytes 1048576
  71.4 0.6 copy.18
  (1 shorter events, 0.0 us)
Async XLA Ops:
  0.6 69.3 %copy-start = (f32[90,2048]{1,0:T(8,128)S(1)}, f32[90,2048]{1,0:T(8,128)}, u32[]{:S(2)}) copy-start(f32[90,2048]{1,0:T(8,128)} %pts_ref.1) | copy-start | bytes 2211844
  0.6 69.3 %copy-start.1 = (bf16[64,2048]{1,0:T(8,128)(2,1)S(1)}, bf16[64,2048]{1,0:T(8,128)(2,1)}, u32[]{:S(2)}) copy-start(bf16[64,2048]{1,0:T(8,128)(2,1)} %left_ref.1) | copy-start | bytes 786436
  0.6 69.3 %copy-start.2 = (bf16[64,256]{1,0:T(8,128)(2,1)S(1)}, bf16[64,256]{1,0:T(8,128)(2,1)}, u32[]{:S(2)}) copy-start(bf16[64,256]{1,0:T(8,128)(2,1)} %right_ref.1) | copy-start | bytes 98308
  69.9 0.7 copy-start.3
  69.9 0.7 copy-start.4
where the time goes:
time: 73.5 us; the launch traced here: 72 us
  Pallas kernels  68.6 us (93%)
  local copies, waits for them, and re-layouts  2.07 us (3%)
  between operations  1.33 us (2%)
    pallas_call x1, Pallas kernels, fused(): pl.pallas_call(functools.partial(fused_kernel, rounds), out_shape=(jax.Sh...  68.6 us
    unnamed x12, local copies, waits for them, and re-layouts  2.07 us

commit v1 on v0

--- a/solution.py
+++ b/solution.py
@@ -19,8 +19,6 @@
 CHIPS = 16
 SLOTS = 48
 PER = 8
-TILE_I = 512
-WIDE = 3
 PART = HERE // 4
 VMEM_LIMIT = 56 * 2**20
 
@@ -33,8 +31,9 @@
 
 
 def fused_kernel(
-    rounds, pts_ref, inv_ref, idx_ref, left_ref, right_ref,
-    point_ref, centre_ref, flag_ref,
+    rounds, pts_hbm, inv_hbm, idx_hbm, left_hbm, right_hbm,
+    point_hbm, centre_hbm, flag_hbm,
+    pts_ref, inv_ref, point_ref, centre_ref, flag_ref, load_sem, store_sem,
     idx_all, rank_all, cols_s, cols_l, lookup, rows_out, rows_in,
     tables, lefts, blocks, rights, point_acc, own_part, to_home, at_home,
     pair_out, pair_in, x_out, x_in, z_out, z_in, back_out, back_in,
@@ -70,6 +69,16 @@
 
         lax.fori_loop(first, last, step, 0)
 
+    loads = [
+        pltpu.make_async_copy(source, here, load_sem.at[number])
+        for number, (source, here) in enumerate((
+            (idx_hbm, idx_all.at[chip]), (right_hbm, rights.at[chip]), (pts_hbm, pts_ref),
+            (inv_hbm, inv_ref), (left_hbm, lefts.at[0]),
+        ))
+    ]
+    for load in loads:
+        load.start()
+
     barrier = pltpu.get_barrier_semaphore()
     pl.semaphore_signal(barrier, inc=1, device_id=across, device_id_type=MESH)
     for dx in (1, 2, 3):
@@ -84,13 +93,14 @@
         return remote(src, dst, send.at[m], recv, {"pts": chip_at(m) * 2 + core})
 
     def idx_copy(m):
-        return rail(idx_ref, idx_all.at[chip], idx_send, idx_recv.at[chip], m)
+        return rail(idx_all.at[chip], idx_all.at[chip], idx_send, idx_recv.at[chip], m)
 
     def idx_arrival(m):
-        return rail(idx_ref, idx_all.at[chip_at(m)], idx_send, idx_recv.at[chip_at(m)], m)
-
+        there = chip_at(m)
+        return rail(idx_all.at[chip], idx_all.at[there], idx_send, idx_recv.at[there], m)
+
+    loads[0].wait()
     loop(1, CHIPS, lambda m: idx_copy(m).start())
-    idx_all[chip] = idx_ref[...]
 
     class Spread:
         def __init__(self, held, send, recv):
@@ -124,8 +134,10 @@
 
     right_spread = Spread(rights, right_send, right_recv)
     block_spread = Spread(blocks, block_send, block_recv)
-    rights[chip] = right_ref[...]
+    loads[1].wait()
     right_spread.first()
+    loads[2].wait()
+    loads[3].wait()
 
     eye = lax.broadcasted_iota(I32, (FEAT, FEAT), 0) == lax.broadcasted_iota(I32, (FEAT, FEAT), 1)
     scale = jnp.sum(jnp.where(eye, inv_ref[...], 0.0), axis=1, keepdims=True)
@@ -157,15 +169,15 @@
         tables[0, span, 128:256] = (turned - upper.astype(F32)).astype(BF16)
     swap_table = remote(tables.at[0], tables.at[1], pair_send.at[1], pair_recv.at[1], pair)
     swap_table.start()
-    swap_left = remote(left_ref, lefts.at[1], pair_send.at[2], pair_recv.at[2], pair)
+    loads[4].wait()
+    swap_left = remote(lefts.at[0], lefts.at[1], pair_send.at[2], pair_recv.at[2], pair)
     swap_left.start()
-    lefts[0] = left_ref[...]
 
     earlier = (
         lax.broadcasted_iota(I32, (BLK, BLK), 0) < lax.broadcasted_iota(I32, (BLK, BLK), 1)
     ).astype(F32).astype(BF16)
 
-    own_owner = idx_ref[...] >> 12
+    own_owner = idx_all[chip] >> 12
     own_hits = jnp.where(
         lax.broadcasted_iota(I32, (CHIPS, BLK), 0) == own_owner, 1.0, 0.0
     )
@@ -271,7 +283,7 @@
     def home_copy(m):
         return rail(to_home.at[m], at_home.at[m], home_send, home_recv.at[m], m)
 
-    def multiply(numbers):
+    def multiply(numbers, last=None):
         blank = jnp.zeros((128 - ROWS, BLK), BF16)
         sides, mates = [], []
         for m in numbers:
@@ -281,65 +293,87 @@
             mates.append(rights[there])
         side = sides[0] if len(sides) == 1 else jnp.concatenate(sides, axis=1)
         mate = mates[0] if len(mates) == 1 else jnp.concatenate(mates, axis=1)
+        def tile(own, span):
+            power = jnp.dot(tables[own, span, :], side, preferred_element_type=F32)
+            kernel = jnp.exp2(jnp.minimum(power, 0.0)).astype(BF16)
+            point_acc[own, :, span] += lax.dot_general(
+                mate, kernel, (((1,), (1,)), ((), ())), preferred_element_type=F32
+            )
+            return jnp.dot(lefts[own, :, span], kernel, preferred_element_type=F32)
+
         total = None
-        for own in range(2):
-            for t in range(HERE // TILE_I):
-                span = slice(t * TILE_I, (t + 1) * TILE_I)
-                power = jnp.dot(tables[own, span, :], side, preferred_element_type=F32)
-                kernel = jnp.exp2(jnp.minimum(power, 0.0)).astype(BF16)
-                point_acc[own, :, span] += lax.dot_general(
-                    mate, kernel, (((1,), (1,)), ((), ())), preferred_element_type=F32
-                )
-                part = jnp.dot(lefts[own, :, span], kernel, preferred_element_type=F32)
+        for own in (1, 0):
+            for t in range(4):
+                span = part_of(t + 1) if last and own == 0 else slice(t * PART, (t + 1) * PART)
+                part = tile(own, span)
                 total = part if total is None else total + part
+                if last:
+                    last(own, t)
         return total
+
+    def part_of(step):
+        return pl.ds(pl.multiple_of(lax.rem(x + step, 4) * PART, PART), PART)
+
+    swap_points = remote(pair_out, pair_in, pair_send.at[3], pair_recv.at[3], pair)
+    swap_flag = remote(flag_mine.at[0], flag_pair, pair_send.at[4], pair_recv.at[4], pair)
+
+    def x_copy(dx):
+        return remote(
+            x_out.at[dx - 1], x_in.at[dx - 1], x_send.at[dx - 1], x_recv.at[dx - 1], along_x(dx)
+        )
+
+    def send_x(dx):
+        span = part_of(dx)
+        x_out[dx - 1] = (point_acc[0, :, span] + pair_in[:, span].astype(F32)).astype(BF16)
+        x_copy(dx).start()
+
+    def leave(own, t):
+        if (own, t) == (1, 3):
+            pair_out[...] = point_acc[1].astype(BF16)
+            swap_points.start()
+            swap_flag.start()
+        if (own, t) == (0, 1):
+            swap_points.wait_recv()
+            send_x(1)
+            send_x(2)
+        if (own, t) == (0, 2):
+            send_x(3)
 
     own_part[...] = multiply([0])
     block_spread.second()
 
-    def advance(number):
-        later = (number + 4) // 5
-        numbers = [
-            (1 - later) * (u + 1) + later * (number - 1 + 4 * (u + 1)) for u in range(WIDE)
-        ]
-
-        @pl.when(number > 0)
-        def _():
-            for m in numbers:
-                right_spread.arrive(m)
-                block_spread.arrive(m)
-
-        total = multiply(numbers)
+    def send_home(total, numbers):
         for u, m in enumerate(numbers):
             to_home[m] = total[:, u * BLK:(u + 1) * BLK].astype(BF16)
             home_copy(m).start()
 
-    loop(0, (CHIPS - 1) // WIDE, advance)
-
-    pair_out[...] = point_acc[1].astype(BF16)
-    swap_points = remote(pair_out, pair_in, pair_send.at[3], pair_recv.at[3], pair)
-    swap_points.start()
-    swap_flag = remote(flag_mine.at[0], flag_pair, pair_send.at[4], pair_recv.at[4], pair)
-    swap_flag.start()
-
-    def x_copy(dx):
-        return remote(
-            x_out.at[dx - 1], x_in.at[dx - 1], x_send.at[dx - 1], x_recv.at[dx - 1], along_x(dx)
-        )
+    def arrive(numbers):
+        for m in numbers:
+            right_spread.arrive(m)
+            block_spread.arrive(m)
+
+    def advance(number):
+        later = (number + 3) // 4
+        numbers = [
+            (1 - later) * (u + 1) + later * (number - 1 + 4 * (u + 1)) for u in range(3)
+        ]
+
+        @pl.when(number > 0)
+        def _():
+            arrive(numbers)
+
+        send_home(multiply(numbers), numbers)
+
+    loop(0, 4, advance)
+    numbers = [7, 11, 15]
+    arrive(numbers)
+    send_home(multiply(numbers, leave), numbers)
 
     def flag_x_copy(dx):
         return remote(
             flag_mine.at[1], flag_x.at[dx - 1], fx_send.at[dx - 1], fx_recv.at[dx - 1], along_x(dx)
         )
 
-    def part_of(step):
-        return pl.ds(pl.multiple_of(lax.rem(x + step, 4) * PART, PART), PART)
-
-    swap_points.wait_recv()
-    for dx in (1, 2, 3):
-        span = part_of(dx)
-        x_out[dx - 1] = (point_acc[0, :, span] + pair_in[:, span].astype(F32)).astype(BF16)
-        x_copy(dx).start()
     swap_flag.wait_recv()
     flag_mine[1] = jnp.maximum(flag_mine[0], flag_pair[...])
     for dx in (1, 2, 3):
@@ -380,6 +414,22 @@
     point_ref[:, mine] = back_out[...].astype(F32)
     flag_across.wait_recv()
     flag_ref[...] = jnp.maximum(flag_mine[2], flag_z[...])[0:1, 0:1]
+    stores = [
+        pltpu.make_async_copy(centre_ref, centre_hbm, store_sem.at[4]),
+        pltpu.make_async_copy(flag_ref, flag_hbm, store_sem.at[5]),
+    ]
+    for store in stores:
+        store.start()
+
+    def store_part(step):
+        span = part_of(step)
+        store = pltpu.make_async_copy(
+            point_ref.at[:, span], point_hbm.at[:, span], store_sem.at[step]
+        )
+        store.start()
+        stores.append(store)
+
+    store_part(0)
 
     def drain(m):
         idx_copy(m).wait_send()
@@ -398,12 +448,15 @@
     for dx in (1, 2, 3):
         back_copy(dx).wait_recv()
         point_ref[:, part_of(4 - dx)] = back_in[dx - 1].astype(F32)
+        store_part(4 - dx)
     for dx in (1, 2, 3):
         back_copy(dx).wait_send()
+    for store in stores:
+        store.wait()
 
 
 def fused(rounds, points, centre_index, inv_scale, left_cols, right_cols):
-    vmem = pl.BlockSpec(memory_space=pltpu.VMEM)
+    anywhere = pl.BlockSpec(memory_space=pl.ANY)
     dma = pltpu.SemaphoreType.DMA
     buf = pltpu.VMEM
     return pl.pallas_call(
@@ -413,9 +466,16 @@
             jax.ShapeDtypeStruct((COLS, BLK), F32),
             jax.ShapeDtypeStruct((1, 1), F32),
         ),
-        in_specs=[vmem] * 5,
-        out_specs=[vmem] * 3,
+        in_specs=[anywhere] * 5,
+        out_specs=[anywhere] * 3,
         scratch_shapes=[
+            buf((FEAT, HERE), F32),
+            buf((1, FEAT), F32),
+            buf((COLS, HERE), F32),
+            buf((COLS, BLK), F32),
+            buf((1, 1), F32),
+            dma((5,)),
+            dma((6,)),
             buf((CHIPS, 1, BLK), I32),
             buf((CHIPS, 1, BLK), F32),
             buf((128, HERE), F32),

time: 73.5 us -> 68.4 us (0.931); the launches traced: 72 us -> 68.3 us
  Pallas kernels: 68.6 us -> 64.9 us
    pallas_call x1, Pallas kernels: 68.6 us -> 64.9 us  [fused(): pl.pallas_call(functools.partial(fused_kernel, rounds), out_shape=(jax.Sh...]
where the time goes in v1:
time: 68.4 us; the launch traced here: 68.3 us
  Pallas kernels  64.9 us (95%)
  local copies, waits for them, and re-layouts  2.07 us (3%)
  between operations  1.33 us (2%)
    pallas_call x1, Pallas kernels, fused(): pl.pallas_call(functools.partial(fused_kernel, rounds), out_shape=(jax.Sh...  64.9 us
    unnamed x12, local copies, waits for them, and re-layouts  2.07 us

profile of v1, /device:TPU:4, one launch (start us, length us, event | category | flops | bytes accessed | tf_op | source)
XLA Modules:
  0.0 68.3 jit_solution(2717081792491722833)
XLA Ops:
  0.6 0.0 copy-start
  0.6 0.0 copy-start.1
  0.6 0.0 copy-start.2
  0.7 64.9 %nystrom_products_1.1 = (f32[64,2048]{1,0:T(8,128)S(1)}, f32[64,256]{1,0:T(8,128)S(1)}, f32[1,1]{1,0:T(1,128)}) custom-call(f32[90,2048]{1,0:T(8,128)} %pts_hbm.1, f32[1,90]{1,0:T(1,128)} %bitcast.7, s32[1,256]{1,0:T(1,128)} %bitcast.5, bf16[64,2048]{1,0:T(8,128)(2,1)} %left_hbm.1, bf16[64,256]{1,0:T(8,128)(2,1)} %right_hbm.1), custom_call_target="tpu_custom_call" | custom-call | tf_op jit(solution)/shard_map/nystrom_products_1/pallas_call | solution.py:462
  66.2 0.0 copy-start.3
  66.2 0.0 copy-start.4
  66.2 0.0 copy-done
  66.2 0.0 copy-done.1
  66.2 0.0 copy-done.2
  66.2 0.6 copy-done.3
  66.8 0.0 copy-done.4
  66.8 0.8 %copy.17 = f32[64,2048]{1,0:T(8,128)} copy(f32[64,2048]{1,0:T(8,128)S(1)} %get-tuple-element.39) | data formatting | bytes 1048576
  67.6 0.6 copy.18
  (1 shorter events, 0.0 us)
Async XLA Ops:
  0.6 65.6 %copy-start = (f32[90,2048]{1,0:T(8,128)S(1)}, f32[90,2048]{1,0:T(8,128)}, u32[]{:S(2)}) copy-start(f32[90,2048]{1,0:T(8,128)} %pts_hbm.1) | copy-start | bytes 2211844
  0.6 65.6 %copy-start.1 = (bf16[64,2048]{1,0:T(8,128)(2,1)S(1)}, bf16[64,2048]{1,0:T(8,128)(2,1)}, u32[]{:S(2)}) copy-start(bf16[64,2048]{1,0:T(8,128)(2,1)} %left_hbm.1) | copy-start | bytes 786436
  0.6 65.6 %copy-start.2 = (bf16[64,256]{1,0:T(8,128)(2,1)S(1)}, bf16[64,256]{1,0:T(8,128)(2,1)}, u32[]{:S(2)}) copy-start(bf16[64,256]{1,0:T(8,128)(2,1)} %right_hbm.1) | copy-start | bytes 98308
  66.2 0.7 copy-start.3
  66.2 0.7 copy-start.4

commit v2 on v1

--- a/solution.py
+++ b/solution.py
@@ -20,6 +20,7 @@
 SLOTS = 48
 PER = 8
 PART = HERE // 4
+HALF = PART // 2
 VMEM_LIMIT = 56 * 2**20
 
 
@@ -33,10 +34,10 @@
 def fused_kernel(
     rounds, pts_hbm, inv_hbm, idx_hbm, left_hbm, right_hbm,
     point_hbm, centre_hbm, flag_hbm,
-    pts_ref, inv_ref, point_ref, centre_ref, flag_ref, load_sem, store_sem,
-    idx_all, rank_all, cols_s, cols_l, lookup, rows_out, rows_in,
-    tables, lefts, blocks, rights, point_acc, own_part, to_home, at_home,
-    pair_out, pair_in, x_out, x_in, z_out, z_in, back_out, back_in,
+    pts_ref, inv_ref, centre_ref, flag_ref, load_sem, store_sem,
+    idx_all, rank_all, cols_s, lookup, rows_out, rows_in,
+    lefts, blocks, rights, point_acc, own_part, to_home, at_home,
+    pair_out, pair_in, x_out, x_in, z_out, z_in, back_out,
     flag_mine, flag_pair, flag_x, flag_z,
     idx_send, idx_recv, row_send, row_recv, right_send, right_recv,
     block_send, block_recv, home_send, home_recv, pair_send, pair_recv,
@@ -112,8 +113,9 @@
 
         def first(self):
             for d in (1, 2, 3):
+                self.copy(d, 0).start()
+            for d in (1, 2, 3):
                 self.copy(4 * d, 0).start()
-                self.copy(d, 0).start()
 
         def second(self):
             for dz in (1, 2, 3):
@@ -142,33 +144,20 @@
     eye = lax.broadcasted_iota(I32, (FEAT, FEAT), 0) == lax.broadcasted_iota(I32, (FEAT, FEAT), 1)
     scale = jnp.sum(jnp.where(eye, inv_ref[...], 0.0), axis=1, keepdims=True)
     scaled = (pts_ref[...] * scale).astype(BF16).astype(F32)
-    half_norm = jnp.sum(scaled * scaled, axis=0, keepdims=True) * (-0.5 * LOG2E)
-    ones = jnp.ones((3, HERE), F32)
+    half_norm = jnp.sum(scaled * scaled, axis=0, keepdims=True) * -0.5
     cols_s[ROWS:, :] = jnp.zeros((128 - ROWS, HERE), F32)
-    cols_l[ROWS:, :] = jnp.zeros((128 - ROWS, HERE), F32)
     cols_s[0:FEAT, :] = scaled
-    cols_l[0:FEAT, :] = scaled * LOG2E
-    cols_s[FEAT:FEAT + 3, :] = ones
-    cols_l[FEAT + 3:ROWS, :] = ones
+    cols_s[FEAT:FEAT + 3, :] = jnp.ones((3, HERE), F32)
     for place, piece in enumerate(pieces(half_norm)):
         cols_s[FEAT + 3 + place:FEAT + 4 + place, :] = piece
-        cols_l[FEAT + place:FEAT + 1 + place, :] = piece
     for part in range(HERE // 128):
         span = slice(part * 128, (part + 1) * 128)
         high, low = part // 2, (part % 2) * 128
-        lookup[core, low:low + 128, high * 128:(high + 1) * 128] = cols_s[:, span].T.astype(BF16)
+        lookup[core, high, low:low + 128, :] = cols_s[:, span].T.astype(BF16)
     swap_lookup = remote(
         lookup.at[core], lookup.at[core], pair_send.at[0], pair_recv.at[0], pair
     )
     swap_lookup.start()
-    for part in range(HERE // 128):
-        span = slice(part * 128, (part + 1) * 128)
-        turned = cols_l[:, span].T
-        upper = turned.astype(BF16)
-        tables[0, span, 0:128] = upper
-        tables[0, span, 128:256] = (turned - upper.astype(F32)).astype(BF16)
-    swap_table = remote(tables.at[0], tables.at[1], pair_send.at[1], pair_recv.at[1], pair)
-    swap_table.start()
     loads[4].wait()
     swap_left = remote(lefts.at[0], lefts.at[1], pair_send.at[2], pair_recv.at[2], pair)
     swap_left.start()
@@ -233,7 +222,8 @@
         high = jnp.concatenate(highs, axis=0)
         rows = jnp.zeros((PER * SLOTS, 128), F32)
         for half in range(2):
-            found = jnp.dot(pick, lookup[half], preferred_element_type=F32)
+            table = jnp.concatenate([lookup[half, h] for h in range(8)], axis=1)
+            found = jnp.dot(pick, table, preferred_element_type=F32)
             for h in range(8):
                 rows = jnp.where(high == half * 8 + h, found[:, h * 128:(h + 1) * 128], rows)
         rows = rows.astype(BF16)
@@ -274,10 +264,14 @@
             rows_in[turn].reshape(CHIPS * SLOTS, 128), placed[turn],
             (((0,), (0,)), ((), ())), preferred_element_type=F32,
         )
-    blocks[chip] = centres[0:ROWS, :].astype(BF16)
+    here = slice(0, BLK)
+    cols_s[0:ROWS, here] = centres[0:ROWS, :]
+    norm_rows = cols_s[FEAT + 3:ROWS, here]
+    cols_s[FEAT + 3:ROWS, here] = cols_s[FEAT:FEAT + 3, here]
+    cols_s[FEAT:FEAT + 3, here] = norm_rows
+    blocks[chip] = cols_s[0:ROWS, here].astype(BF16)
 
     block_spread.first()
-    swap_table.wait_recv()
     swap_left.wait_recv()
 
     def home_copy(m):
@@ -289,12 +283,14 @@
         for m in numbers:
             there = chip_at(m)
             cut = blocks[there]
-            sides.append(jnp.concatenate([cut, blank, cut, blank], axis=0))
+            sides.append(jnp.concatenate([cut, blank], axis=0))
             mates.append(rights[there])
         side = sides[0] if len(sides) == 1 else jnp.concatenate(sides, axis=1)
         mate = mates[0] if len(mates) == 1 else jnp.concatenate(mates, axis=1)
-        def tile(own, span):
-            power = jnp.dot(tables[own, span, :], side, preferred_element_type=F32)
+        def tile(own, q, span):
+            holder = core if own == 0 else 1 - core
+            rows = jnp.concatenate([lookup[holder, 2 * q], lookup[holder, 2 * q + 1]], axis=0)
+            power = jnp.dot(rows, side, preferred_element_type=F32) * LOG2E
             kernel = jnp.exp2(jnp.minimum(power, 0.0)).astype(BF16)
             point_acc[own, :, span] += lax.dot_general(
                 mate, kernel, (((1,), (1,)), ((), ())), preferred_element_type=F32
@@ -304,8 +300,10 @@
         total = None
         for own in (1, 0):
             for t in range(4):
-                span = part_of(t + 1) if last and own == 0 else slice(t * PART, (t + 1) * PART)
-                part = tile(own, span)
+                if last and own == 0:
+                    part = tile(own, lax.rem(x + t + 1, 4), part_of(t + 1))
+                else:
+                    part = tile(own, t, slice(t * PART, (t + 1) * PART))
                 total = part if total is None else total + part
                 if last:
                     last(own, t)
@@ -317,15 +315,24 @@
     swap_points = remote(pair_out, pair_in, pair_send.at[3], pair_recv.at[3], pair)
     swap_flag = remote(flag_mine.at[0], flag_pair, pair_send.at[4], pair_recv.at[4], pair)
 
-    def x_copy(dx):
+    def half_of(step, half):
+        start = lax.rem(x + step, 4) * PART + half * HALF
+        return pl.ds(pl.multiple_of(start, HALF), HALF)
+
+    def x_copy(dx, half):
         return remote(
-            x_out.at[dx - 1], x_in.at[dx - 1], x_send.at[dx - 1], x_recv.at[dx - 1], along_x(dx)
-        )
+            x_out.at[dx - 1, half], x_in.at[dx - 1, half],
+            x_send.at[dx - 1, half], x_recv.at[dx - 1, half], along_x(dx),
+        )
+
+    def chip_sum(dx, half):
+        span = half_of(dx, half)
+        return point_acc[0, :, span] + pair_in[:, span].astype(F32)
 
     def send_x(dx):
-        span = part_of(dx)
-        x_out[dx - 1] = (point_acc[0, :, span] + pair_in[:, span].astype(F32)).astype(BF16)
-        x_copy(dx).start()
+        for half in range(2):
+            x_out[dx - 1, half] = chip_sum(dx, half).astype(BF16)
+            x_copy(dx, half).start()
 
     def leave(own, t):
         if (own, t) == (1, 3):
@@ -355,7 +362,7 @@
     def advance(number):
         later = (number + 3) // 4
         numbers = [
-            (1 - later) * (u + 1) + later * (number - 1 + 4 * (u + 1)) for u in range(3)
+            (1 - later) * (u + 1) + later * (number + 4 * (u + 1)) for u in range(3)
         ]
 
         @pl.when(number > 0)
@@ -365,7 +372,7 @@
         send_home(multiply(numbers), numbers)
 
     loop(0, 4, advance)
-    numbers = [7, 11, 15]
+    numbers = [4, 8, 12]
     arrive(numbers)
     send_home(multiply(numbers, leave), numbers)
 
@@ -379,20 +386,23 @@
     for dx in (1, 2, 3):
         flag_x_copy(dx).start()
 
-    mine = part_of(0)
-    total = point_acc[0, :, mine] + pair_in[:, mine].astype(F32)
     worst = flag_mine[1]
-    for dx in (1, 2, 3):
-        x_copy(dx).wait_recv()
-        total = total + x_in[dx - 1].astype(F32)
-    z_out[...] = total.astype(BF16)
-    swap_z = remote(z_out, z_in, z_send.at[0], z_recv.at[0], across)
-    swap_z.start()
+    swap_z = [
+        remote(z_out.at[half], z_in.at[half], z_send.at[half], z_recv.at[half], across)
+        for half in range(2)
+    ]
+    for half in range(2):
+        total = chip_sum(0, half)
+        for dx in (1, 2, 3):
+            x_copy(dx, half).wait_recv()
+            total = total + x_in[dx - 1, half].astype(F32)
+        z_out[half] = total.astype(BF16)
+        swap_z[half].start()
     for dx in (1, 2, 3):
         flag_x_copy(dx).wait_recv()
         worst = jnp.maximum(worst, flag_x[dx - 1])
     flag_mine[2] = worst
-    flag_across = remote(flag_mine.at[2], flag_z, z_send.at[1], z_recv.at[1], across)
+    flag_across = remote(flag_mine.at[2], flag_z, z_send.at[2], z_recv.at[2], across)
     flag_across.start()
 
     loop(1, CHIPS, lambda m: home_copy(m).wait_recv())
@@ -401,36 +411,30 @@
         centre = centre + at_home[m].astype(F32)
     centre_ref[...] = centre
 
-    swap_z.wait_recv()
-    back_out[...] = (z_out[...].astype(F32) + z_in[...].astype(F32)).astype(BF16)
-
-    def back_copy(dx):
+    def back_copy(dx, half):
         return remote(
-            back_out, back_in.at[dx - 1], back_send.at[dx - 1], back_recv.at[dx - 1], along_x(dx)
-        )
-
-    for dx in (1, 2, 3):
-        back_copy(dx).start()
-    point_ref[:, mine] = back_out[...].astype(F32)
+            back_out.at[half], point_hbm.at[:, half_of(0, half)],
+            back_send.at[dx - 1, half], back_recv.at[dx - 1, half], along_x(dx),
+        )
+
+    stores = []
+    for half in range(2):
+        swap_z[half].wait_recv()
+        back_out[half] = (z_out[half].astype(F32) + z_in[half].astype(F32)).astype(BF16)
+        for dx in (1, 2, 3):
+            back_copy(dx, half).start()
+        stores.append(pltpu.make_async_copy(
+            back_out.at[half], point_hbm.at[:, half_of(0, half)], store_sem.at[half]
+        ))
     flag_across.wait_recv()
     flag_ref[...] = jnp.maximum(flag_mine[2], flag_z[...])[0:1, 0:1]
-    stores = [
+    stores += [
         pltpu.make_async_copy(centre_ref, centre_hbm, store_sem.at[4]),
         pltpu.make_async_copy(flag_ref, flag_hbm, store_sem.at[5]),
     ]
     for store in stores:
         store.start()
 
-    def store_part(step):
-        span = part_of(step)
-        store = pltpu.make_async_copy(
-            point_ref.at[:, span], point_hbm.at[:, span], store_sem.at[step]
-        )
-        store.start()
-        stores.append(store)
-
-    store_part(0)
-
     def drain(m):
         idx_copy(m).wait_send()
         right_spread.drain(m)
@@ -439,18 +443,20 @@
 
     loop(1, CHIPS, drain)
     each_round(lambda turn, m: row_copy(turn, m).wait_send())
-    for copy in (swap_lookup, swap_table, swap_left, swap_points, swap_flag, swap_z, flag_across):
+    for copy in (swap_lookup, swap_left, swap_points, swap_flag, *swap_z, flag_across):
         copy.wait_send()
     for dx in (1, 2, 3):
-        x_copy(dx).wait_send()
+        for half in range(2):
+            x_copy(dx, half).wait_send()
         flag_x_copy(dx).wait_send()
 
-    for dx in (1, 2, 3):
-        back_copy(dx).wait_recv()
-        point_ref[:, part_of(4 - dx)] = back_in[dx - 1].astype(F32)
-        store_part(4 - dx)
-    for dx in (1, 2, 3):
-        back_copy(dx).wait_send()
+    for half in range(2):
+        for dx in (1, 2, 3):
+            remote(
+                back_out.at[half], point_hbm.at[:, half_of(4 - dx, half)],
+                back_send.at[dx - 1, half], back_recv.at[dx - 1, half], along_x(dx),
+            ).wait_recv()
+            back_copy(dx, half).wait_send()
     for store in stores:
         store.wait()
 
@@ -462,7 +468,7 @@
     return pl.pallas_call(
         functools.partial(fused_kernel, rounds),
         out_shape=(
-            jax.ShapeDtypeStruct((COLS, HERE), F32),
+            jax.ShapeDtypeStruct((COLS, HERE), BF16),
             jax.ShapeDtypeStruct((COLS, BLK), F32),
             jax.ShapeDtypeStruct((1, 1), F32),
         ),
@@ -471,7 +477,6 @@
         scratch_shapes=[
             buf((FEAT, HERE), F32),
             buf((1, FEAT), F32),
-            buf((COLS, HERE), F32),
             buf((COLS, BLK), F32),
             buf((1, 1), F32),
             dma((5,)),
@@ -479,11 +484,9 @@
             buf((CHIPS, 1, BLK), I32),
             buf((CHIPS, 1, BLK), F32),
             buf((128, HERE), F32),
-            buf((128, HERE), F32),
-            buf((2, 256, 1024), BF16),
+            buf((2, 8, 256, 128), BF16),
             buf((rounds, CHIPS, SLOTS, 128), BF16),
             buf((rounds, CHIPS, SLOTS, 128), BF16),
-            buf((2, HERE, 256), BF16),
             buf((2, COLS, HERE), BF16),
             buf((CHIPS, ROWS, BLK), BF16),
             buf((CHIPS, COLS, BLK), BF16),
@@ -493,12 +496,11 @@
             buf((CHIPS, COLS, BLK), BF16),
             buf((COLS, HERE), BF16),
             buf((COLS, HERE), BF16),
-            buf((3, COLS, PART), BF16),
-            buf((3, COLS, PART), BF16),
-            buf((COLS, PART), BF16),
-            buf((COLS, PART), BF16),
-            buf((COLS, PART), BF16),
-            buf((3, COLS, PART), BF16),
+            buf((3, 2, COLS, HALF), BF16),
+            buf((3, 2, COLS, HALF), BF16),
+            buf((2, COLS, HALF), BF16),
+            buf((2, COLS, HALF), BF16),
+            buf((2, COLS, HALF), BF16),
             buf((3, 8, 128), F32),
             buf((8, 128), F32),
             buf((3, 8, 128), F32),
@@ -507,8 +509,9 @@
         + [dma((CHIPS,))] * 2
         + [dma((rounds, CHIPS))] * 2
         + [dma((CHIPS,))] * 6
-        + [dma((5,)), dma((5,)), dma((3,)), dma((3,)), dma((2,)), dma((2,))]
-        + [dma((3,))] * 4,
+        + [dma((5,)), dma((5,)), dma((3, 2)), dma((3, 2)), dma((3,)), dma((3,))]
+        + [dma((3, 2))] * 2
+        + [dma((3,))] * 2,
         compiler_params=pltpu.CompilerParams(
             collective_id=rounds, has_side_effects=True, vmem_limit_bytes=VMEM_LIMIT
         ),
@@ -521,9 +524,10 @@
 
 def body(*arguments):
     point_side, centre_side, most = fused(1, *arguments)
-    return lax.cond(
+    point_side, centre_side = lax.cond(
         most[0, 0] > SLOTS, lambda: fused(ROUNDS, *arguments)[:2], lambda: (point_side, centre_side)
     )
+    return point_side.astype(F32), centre_side
 
 
 def solution(mesh):

time: 68.4 us -> 67.1 us (0.981)
  Pallas kernels: 64.9 us -> 63.3 us
  other arithmetic: 0 us -> 0.83 us
  local copies, waits for them, and re-layouts: 2.07 us -> 1.28 us
    pallas_call x1, Pallas kernels: 64.9 us -> 63.3 us  [fused(): pl.pallas_call(functools.partial(fused_kernel, rounds), out_shape=(jax.Sh...]
    convert_element_type x0 -> x1, other arithmetic: none -> 0.83 us  [body(): return (point_side.astype(F32), centre_side)]
    unnamed x12 -> x11, local copies, waits for them, and re-layouts: 2.07 us -> 1.28 us
where the time goes in v2:
time: 67.1 us; the launch traced here: 66.7 us
  Pallas kernels  63.3 us (94%)
  between operations  1.33 us (2%)
  local copies, waits for them, and re-layouts  1.28 us (2%)
  other arithmetic  0.83 us (1%)
    pallas_call x1, Pallas kernels, fused(): pl.pallas_call(functools.partial(fused_kernel, rounds), out_shape=(jax.Sh...  63.3 us

profile of v2, /device:TPU:4, one launch (start us, length us, event | category | flops | bytes accessed | tf_op | source)
XLA Modules:
  0.0 66.7 jit_solution(11046101585309837231)
XLA Ops:
  0.6 0.0 copy-start
  0.6 0.0 copy-start.1
  0.6 0.0 copy-start.2
  0.7 63.3 %nystrom_products_1.1 = (bf16[64,2048]{1,0:T(8,128)(2,1)S(1)}, f32[64,256]{1,0:T(8,128)S(1)}, f32[1,1]{1,0:T(1,128)}) custom-call(f32[90,2048]{1,0:T(8,128)} %pts_hbm.1, f32[1,90]{1,0:T(1,128)} %bitcast.7, s32[1,256]{1,0:T(1,128)} %bitcast.5, bf16[64,2048]{1,0:T(8,128)(2,1)} %left_hbm.1, bf16[64,256]{1,0:T(8,128)(2,1)} %right_hbm.1), custom_call_target="tpu_custom_call" | custom-call | tf_op jit(solution)/shard_map/nystrom_products_1/pallas_call | solution.py:468
  64.6 0.0 copy-start.3
  64.6 0.0 copy-start.4
  64.6 0.0 copy-done
  64.6 0.0 copy-done.1
  64.6 0.0 copy-done.2
  64.6 0.6 copy-done.3
  65.2 0.0 copy-done.4
  65.2 0.8 %convert_element_type.18 = f32[64,2048]{1,0:T(8,128)} convert(bf16[64,2048]{1,0:T(8,128)(2,1)S(1)} %get-tuple-element.42) | non-fusion elementwise | flops 131072 | bytes 786432 | tf_op jit(solution)/shard_map/convert_element_type | solution.py:530
  66.1 0.6 copy.12
  (1 shorter events, 0.0 us)
Async XLA Ops:
  0.6 64.0 %copy-start = (f32[90,2048]{1,0:T(8,128)S(1)}, f32[90,2048]{1,0:T(8,128)}, u32[]{:S(2)}) copy-start(f32[90,2048]{1,0:T(8,128)} %pts_hbm.1) | copy-start | bytes 2211844
  0.6 64.0 %copy-start.1 = (bf16[64,2048]{1,0:T(8,128)(2,1)S(1)}, bf16[64,2048]{1,0:T(8,128)(2,1)}, u32[]{:S(2)}) copy-start(bf16[64,2048]{1,0:T(8,128)(2,1)} %left_hbm.1) | copy-start | bytes 786436
  0.6 64.0 %copy-start.2 = (bf16[64,256]{1,0:T(8,128)(2,1)S(1)}, bf16[64,256]{1,0:T(8,128)(2,1)}, u32[]{:S(2)}) copy-start(bf16[64,256]{1,0:T(8,128)(2,1)} %right_hbm.1) | copy-start | bytes 98308
  64.6 0.7 %copy-start.3 = (s32[256]{0:T(256)S(1)}, s32[256]{0:T(256)}, u32[]{:S(2)}) copy-start(s32[256]{0:T(256)} %param.8) | copy-start | bytes 3076
  64.6 0.7 %copy-start.4 = (f32[90]{0:T(128)S(1)}, f32[90]{0:T(128)}, u32[]{:S(2)}) copy-start(f32[90]{0:T(128)} %param.9) | copy-start | bytes 1084

commit v3 on v2

--- a/solution.py
+++ b/solution.py
@@ -41,7 +41,7 @@
     flag_mine, flag_pair, flag_x, flag_z,
     idx_send, idx_recv, row_send, row_recv, right_send, right_recv,
     block_send, block_recv, home_send, home_recv, pair_send, pair_recv,
-    x_send, x_recv, z_send, z_recv, back_send, back_recv, fx_send, fx_recv,
+    part_send, part_recv, x_send, x_recv, z_send, z_recv, back_send, back_recv, fx_send, fx_recv,
 ):
     me = lax.axis_index("pts")
     panel = lax.axis_index("ctr")
@@ -300,7 +300,7 @@
         total = None
         for own in (1, 0):
             for t in range(4):
-                if last and own == 0:
+                if last:
                     part = tile(own, lax.rem(x + t + 1, 4), part_of(t + 1))
                 else:
                     part = tile(own, t, slice(t * PART, (t + 1) * PART))
@@ -312,7 +312,9 @@
     def part_of(step):
         return pl.ds(pl.multiple_of(lax.rem(x + step, 4) * PART, PART), PART)
 
-    swap_points = remote(pair_out, pair_in, pair_send.at[3], pair_recv.at[3], pair)
+    def swap_part(t):
+        return remote(pair_out.at[t], pair_in.at[t], part_send.at[t], part_recv.at[t], pair)
+
     swap_flag = remote(flag_mine.at[0], flag_pair, pair_send.at[4], pair_recv.at[4], pair)
 
     def half_of(step, half):
@@ -327,7 +329,8 @@
 
     def chip_sum(dx, half):
         span = half_of(dx, half)
-        return point_acc[0, :, span] + pair_in[:, span].astype(F32)
+        arrived = pair_in[(dx + 3) % 4, :, half * HALF:(half + 1) * HALF]
+        return point_acc[0, :, span] + arrived.astype(F32)
 
     def send_x(dx):
         for half in range(2):
@@ -335,16 +338,15 @@
             x_copy(dx, half).start()
 
     def leave(own, t):
+        if own == 1:
+            pair_out[t] = point_acc[1, :, part_of(t + 1)].astype(BF16)
+            swap_part(t).start()
         if (own, t) == (1, 3):
-            pair_out[...] = point_acc[1].astype(BF16)
-            swap_points.start()
             swap_flag.start()
-        if (own, t) == (0, 1):
-            swap_points.wait_recv()
-            send_x(1)
-            send_x(2)
-        if (own, t) == (0, 2):
-            send_x(3)
+        if own == 0:
+            swap_part(t).wait_recv()
+        if own == 0 and t < 3:
+            send_x(t + 1)
 
     own_part[...] = multiply([0])
     block_spread.second()
@@ -443,8 +445,10 @@
 
     loop(1, CHIPS, drain)
     each_round(lambda turn, m: row_copy(turn, m).wait_send())
-    for copy in (swap_lookup, swap_left, swap_points, swap_flag, *swap_z, flag_across):
+    for copy in (swap_lookup, swap_left, swap_flag, *swap_z, flag_across):
         copy.wait_send()
+    for t in range(4):
+        swap_part(t).wait_send()
     for dx in (1, 2, 3):
         for half in range(2):
             x_copy(dx, half).wait_send()
@@ -494,8 +498,8 @@
             buf((COLS, BLK), F32),
             buf((CHIPS, COLS, BLK), BF16),
             buf((CHIPS, COLS, BLK), BF16),
-            buf((COLS, HERE), BF16),
-            buf((COLS, HERE), BF16),
+            buf((4, COLS, PART), BF16),
+            buf((4, COLS, PART), BF16),
             buf((3, 2, COLS, HALF), BF16),
             buf((3, 2, COLS, HALF), BF16),
             buf((2, COLS, HALF), BF16),
@@ -509,7 +513,7 @@
         + [dma((CHIPS,))] * 2
         + [dma((rounds, CHIPS))] * 2
         + [dma((CHIPS,))] * 6
-        + [dma((5,)), dma((5,)), dma((3, 2)), dma((3, 2)), dma((3,)), dma((3,))]
+        + [dma((5,)), dma((5,)), dma((4,)), dma((4,)), dma((3, 2)), dma((3, 2)), dma((3,)), dma((3,))]
         + [dma((3, 2))] * 2
         + [dma((3,))] * 2,
         compiler_params=pltpu.CompilerParams(

time: 67.1 us -> 66.4 us (0.990)
  Pallas kernels: 63.3 us -> 62 us
    pallas_call x1, Pallas kernels: 63.3 us -> 62 us  [fused(): pl.pallas_call(functools.partial(fused_kernel, rounds), out_shape=(jax.Sh...]
where the time goes in v3:
time: 66.4 us; the launch traced here: 65.5 us
  Pallas kernels  62 us (93%)
  between operations  1.33 us (2%)
  local copies, waits for them, and re-layouts  1.28 us (2%)
  other arithmetic  0.83 us (1%)
    pallas_call x1, Pallas kernels, fused(): pl.pallas_call(functools.partial(fused_kernel, rounds), out_shape=(jax.Sh...  62 us

profile of v3, /device:TPU:4, one launch (start us, length us, event | category | flops | bytes accessed | tf_op | source)
XLA Modules:
  0.0 65.5 jit_solution(8336665917333255740)
XLA Ops:
  0.6 0.0 copy-start
  0.6 0.0 copy-start.1
  0.6 0.0 copy-start.2
  0.7 62.0 %nystrom_products_1.1 = (bf16[64,2048]{1,0:T(8,128)(2,1)S(1)}, f32[64,256]{1,0:T(8,128)S(1)}, f32[1,1]{1,0:T(1,128)}) custom-call(f32[90,2048]{1,0:T(8,128)} %pts_hbm.1, f32[1,90]{1,0:T(1,128)} %bitcast.7, s32[1,256]{1,0:T(1,128)} %bitcast.5, bf16[64,2048]{1,0:T(8,128)(2,1)} %left_hbm.1, bf16[64,256]{1,0:T(8,128)(2,1)} %right_hbm.1), custom_call_target="tpu_custom_call" | custom-call | tf_op jit(solution)/shard_map/nystrom_products_1/pallas_call | solution.py:472
  63.3 0.0 copy-start.3
  63.3 0.0 copy-start.4
  63.3 0.0 copy-done
  63.4 0.0 copy-done.1
  63.4 0.0 copy-done.2
  63.4 0.6 copy-done.3
  64.0 0.0 copy-done.4
  64.0 0.8 %convert_element_type.18 = f32[64,2048]{1,0:T(8,128)} convert(bf16[64,2048]{1,0:T(8,128)(2,1)S(1)} %get-tuple-element.42) | non-fusion elementwise | flops 131072 | bytes 786432 | tf_op jit(solution)/shard_map/convert_element_type | solution.py:534
  64.8 0.6 copy.12
  (1 shorter events, 0.0 us)
Async XLA Ops:
  0.6 62.7 %copy-start = (f32[90,2048]{1,0:T(8,128)S(1)}, f32[90,2048]{1,0:T(8,128)}, u32[]{:S(2)}) copy-start(f32[90,2048]{1,0:T(8,128)} %pts_hbm.1) | copy-start | bytes 2211844
  0.6 62.7 %copy-start.1 = (bf16[64,2048]{1,0:T(8,128)(2,1)S(1)}, bf16[64,2048]{1,0:T(8,128)(2,1)}, u32[]{:S(2)}) copy-start(bf16[64,2048]{1,0:T(8,128)(2,1)} %left_hbm.1) | copy-start | bytes 786436
  0.6 62.7 %copy-start.2 = (bf16[64,256]{1,0:T(8,128)(2,1)S(1)}, bf16[64,256]{1,0:T(8,128)(2,1)}, u32[]{:S(2)}) copy-start(bf16[64,256]{1,0:T(8,128)(2,1)} %right_hbm.1) | copy-start | bytes 98308
  63.3 0.7 %copy-start.3 = (s32[256]{0:T(256)S(1)}, s32[256]{0:T(256)}, u32[]{:S(2)}) copy-start(s32[256]{0:T(256)} %param.8) | copy-start | bytes 3076
  63.3 0.7 %copy-start.4 = (f32[90]{0:T(128)S(1)}, f32[90]{0:T(128)}, u32[]{:S(2)}) copy-start(f32[90]{0:T(128)} %param.9) | copy-start | bytes 1084

commit v4 on v3

--- a/solution.py
+++ b/solution.py
@@ -277,17 +277,27 @@
     def home_copy(m):
         return rail(to_home.at[m], at_home.at[m], home_send, home_recv.at[m], m)
 
-    def multiply(numbers, last=None):
+    def send_home(total, numbers):
+        if numbers == [0]:
+            own_part[...] = total
+            return
+        for u, m in enumerate(numbers):
+            to_home[m] = total[:, u * BLK:(u + 1) * BLK].astype(BF16)
+            home_copy(m).start()
+
+    plain = [(0, own, t) for own in (1, 0) for t in range(4)]
+
+    def multiply(sets, order=plain, after=None):
         blank = jnp.zeros((128 - ROWS, BLK), BF16)
         sides, mates = [], []
-        for m in numbers:
-            there = chip_at(m)
-            cut = blocks[there]
-            sides.append(jnp.concatenate([cut, blank], axis=0))
-            mates.append(rights[there])
-        side = sides[0] if len(sides) == 1 else jnp.concatenate(sides, axis=1)
-        mate = mates[0] if len(mates) == 1 else jnp.concatenate(mates, axis=1)
-        def tile(own, q, span):
+        for numbers in sets:
+            places = [chip_at(m) for m in numbers]
+            sides.append(jnp.concatenate(
+                [jnp.concatenate([blocks[there], blank], axis=0) for there in places], axis=1
+            ))
+            mates.append(jnp.concatenate([rights[there] for there in places], axis=1))
+
+        def tile(own, q, span, side, mate):
             holder = core if own == 0 else 1 - core
             rows = jnp.concatenate([lookup[holder, 2 * q], lookup[holder, 2 * q + 1]], axis=0)
             power = jnp.dot(rows, side, preferred_element_type=F32) * LOG2E
@@ -297,17 +307,20 @@
             )
             return jnp.dot(lefts[own, :, span], kernel, preferred_element_type=F32)
 
-        total = None
-        for own in (1, 0):
-            for t in range(4):
-                if last:
-                    part = tile(own, lax.rem(x + t + 1, 4), part_of(t + 1))
-                else:
-                    part = tile(own, t, slice(t * PART, (t + 1) * PART))
-                total = part if total is None else total + part
-                if last:
-                    last(own, t)
-        return total
+        totals = [None for _ in sets]
+        for place, (number, own, t) in enumerate(order):
+            if after:
+                q, span = lax.rem(x + t + 1, 4), part_of(t + 1)
+            else:
+                q, span = t, slice(t * PART, (t + 1) * PART)
+            part = tile(own, q, span, sides[number], mates[number])
+            total = totals[number]
+            totals[number] = part if total is None else total + part
+            if number not in [later[0] for later in order[place + 1:]]:
+                send_home(totals[number], sets[number])
+            if after:
+                after(number, own, t)
+        return totals
 
     def part_of(step):
         return pl.ds(pl.multiple_of(lax.rem(x + step, 4) * PART, PART), PART)
@@ -337,24 +350,18 @@
             x_out[dx - 1, half] = chip_sum(dx, half).astype(BF16)
             x_copy(dx, half).start()
 
-    def leave(own, t):
+    def leave(number, own, t):
         if own == 1:
             pair_out[t] = point_acc[1, :, part_of(t + 1)].astype(BF16)
             swap_part(t).start()
-        if (own, t) == (1, 3):
+        if (own, t) == (1, 0):
             swap_flag.start()
-        if own == 0:
+        if own == 0 and t < 3:
             swap_part(t).wait_recv()
-        if own == 0 and t < 3:
             send_x(t + 1)
 
-    own_part[...] = multiply([0])
+    multiply([[0]])
     block_spread.second()
-
-    def send_home(total, numbers):
-        for u, m in enumerate(numbers):
-            to_home[m] = total[:, u * BLK:(u + 1) * BLK].astype(BF16)
-            home_copy(m).start()
 
     def arrive(numbers):
         for m in numbers:
@@ -371,12 +378,13 @@
         def _():
             arrive(numbers)
 
-        send_home(multiply(numbers), numbers)
+        multiply([numbers])
 
     loop(0, 4, advance)
     numbers = [4, 8, 12]
     arrive(numbers)
-    send_home(multiply(numbers, leave), numbers)
+    order = [(0, own, t) for own in (1, 0) for t in range(3)] + [(0, 1, 3), (0, 0, 3)]
+    multiply([numbers], order, leave)
 
     def flag_x_copy(dx):
         return remote(
@@ -388,6 +396,7 @@
     for dx in (1, 2, 3):
         flag_x_copy(dx).start()
 
+    swap_part(3).wait_recv()
     worst = flag_mine[1]
     swap_z = [
         remote(z_out.at[half], z_in.at[half], z_send.at[half], z_recv.at[half], across)
@@ -407,12 +416,6 @@
     flag_across = remote(flag_mine.at[2], flag_z, z_send.at[2], z_recv.at[2], across)
     flag_across.start()
 
-    loop(1, CHIPS, lambda m: home_copy(m).wait_recv())
-    centre = own_part[...]
-    for m in range(1, CHIPS):
-        centre = centre + at_home[m].astype(F32)
-    centre_ref[...] = centre
-
     def back_copy(dx, half):
         return remote(
             back_out.at[half], point_hbm.at[:, half_of(0, half)],
@@ -428,6 +431,12 @@
         stores.append(pltpu.make_async_copy(
             back_out.at[half], point_hbm.at[:, half_of(0, half)], store_sem.at[half]
         ))
+    loop(1, CHIPS, lambda m: home_copy(m).wait_recv())
+    centre = own_part[...]
+    for m in range(1, CHIPS):
+        centre = centre + at_home[m].astype(F32)
+    centre_ref[...] = centre
+
     flag_across.wait_recv()
     flag_ref[...] = jnp.maximum(flag_mine[2], flag_z[...])[0:1, 0:1]
     stores += [

time: 66.4 us -> 65.8 us (level)
  no operation moved by 1% of the time
where the time goes in v4:
time: 65.8 us; the launch traced here: 65.1 us
  Pallas kernels  61.6 us (94%)
  between operations  1.33 us (2%)
  local copies, waits for them, and re-layouts  1.28 us (2%)
  other arithmetic  0.83 us (1%)
    pallas_call x1, Pallas kernels, fused(): pl.pallas_call(functools.partial(fused_kernel, rounds), out_shape=(jax.Sh...  61.6 us

profile of v4, /device:TPU:4, one launch (start us, length us, event | category | flops | bytes accessed | tf_op | source)
XLA Modules:
  0.0 65.1 jit_solution(9241417960464245484)
XLA Ops:
  0.6 0.0 copy-start
  0.6 0.0 copy-start.1
  0.6 0.0 copy-start.2
  0.7 61.6 %nystrom_products_1.1 = (bf16[64,2048]{1,0:T(8,128)(2,1)S(1)}, f32[64,256]{1,0:T(8,128)S(1)}, f32[1,1]{1,0:T(1,128)}) custom-call(f32[90,2048]{1,0:T(8,128)} %pts_hbm.1, f32[1,90]{1,0:T(1,128)} %bitcast.7, s32[1,256]{1,0:T(1,128)} %bitcast.5, bf16[64,2048]{1,0:T(8,128)(2,1)} %left_hbm.1, bf16[64,256]{1,0:T(8,128)(2,1)} %right_hbm.1), custom_call_target="tpu_custom_call" | custom-call | tf_op jit(solution)/shard_map/nystrom_products_1/pallas_call | solution.py:481
  62.9 0.0 copy-start.3
  62.9 0.0 copy-start.4
  62.9 0.0 copy-done
  63.0 0.0 copy-done.1
  63.0 0.0 copy-done.2
  63.0 0.6 copy-done.3
  63.6 0.0 copy-done.4
  63.6 0.8 %convert_element_type.18 = f32[64,2048]{1,0:T(8,128)} convert(bf16[64,2048]{1,0:T(8,128)(2,1)S(1)} %get-tuple-element.42) | non-fusion elementwise | flops 131072 | bytes 786432 | tf_op jit(solution)/shard_map/convert_element_type | solution.py:543
  64.4 0.6 copy.12
  (1 shorter events, 0.0 us)
Async XLA Ops:
  0.6 62.3 %copy-start = (f32[90,2048]{1,0:T(8,128)S(1)}, f32[90,2048]{1,0:T(8,128)}, u32[]{:S(2)}) copy-start(f32[90,2048]{1,0:T(8,128)} %pts_hbm.1) | copy-start | bytes 2211844
  0.6 62.3 %copy-start.1 = (bf16[64,2048]{1,0:T(8,128)(2,1)S(1)}, bf16[64,2048]{1,0:T(8,128)(2,1)}, u32[]{:S(2)}) copy-start(bf16[64,2048]{1,0:T(8,128)(2,1)} %left_hbm.1) | copy-start | bytes 786436
  0.6 62.3 %copy-start.2 = (bf16[64,256]{1,0:T(8,128)(2,1)S(1)}, bf16[64,256]{1,0:T(8,128)(2,1)}, u32[]{:S(2)}) copy-start(bf16[64,256]{1,0:T(8,128)(2,1)} %right_hbm.1) | copy-start | bytes 98308
  62.9 0.7 %copy-start.3 = (s32[256]{0:T(256)S(1)}, s32[256]{0:T(256)}, u32[]{:S(2)}) copy-start(s32[256]{0:T(256)} %param.8) | copy-start | bytes 3076
  62.9 0.7 %copy-start.4 = (f32[90]{0:T(128)S(1)}, f32[90]{0:T(128)}, u32[]{:S(2)}) copy-start(f32[90]{0:T(128)} %param.9) | copy-start | bytes 1084

commit v5 on v4

--- a/solution.py
+++ b/solution.py
@@ -383,7 +383,7 @@
     loop(0, 4, advance)
     numbers = [4, 8, 12]
     arrive(numbers)
-    order = [(0, own, t) for own in (1, 0) for t in range(3)] + [(0, 1, 3), (0, 0, 3)]
+    order = [(0, own, t) for own in (1, 0) for t in (1, 0, 2)] + [(0, 1, 3), (0, 0, 3)]
     multiply([numbers], order, leave)
 
     def flag_x_copy(dx):

time: 65.8 us -> 65.8 us (level)
  no operation moved by 1% of the time
where the time goes in v5:
time: 65.8 us; the launch traced here: 65 us
  Pallas kernels  61.6 us (94%)
  between operations  1.33 us (2%)
  local copies, waits for them, and re-layouts  1.28 us (2%)
  other arithmetic  0.83 us (1%)
    pallas_call x1, Pallas kernels, fused(): pl.pallas_call(functools.partial(fused_kernel, rounds), out_shape=(jax.Sh...  61.6 us

profile of v5, /device:TPU:4, one launch (start us, length us, event | category | flops | bytes accessed | tf_op | source)
XLA Modules:
  0.0 65.0 jit_solution(2909350883121637764)
XLA Ops:
  0.6 0.0 copy-start
  0.6 0.0 copy-start.1
  0.6 0.0 copy-start.2
  0.7 61.6 %nystrom_products_1.1 = (bf16[64,2048]{1,0:T(8,128)(2,1)S(1)}, f32[64,256]{1,0:T(8,128)S(1)}, f32[1,1]{1,0:T(1,128)}) custom-call(f32[90,2048]{1,0:T(8,128)} %pts_hbm.1, f32[1,90]{1,0:T(1,128)} %bitcast.7, s32[1,256]{1,0:T(1,128)} %bitcast.5, bf16[64,2048]{1,0:T(8,128)(2,1)} %left_hbm.1, bf16[64,256]{1,0:T(8,128)(2,1)} %right_hbm.1), custom_call_target="tpu_custom_call" | custom-call | tf_op jit(solution)/shard_map/nystrom_products_1/pallas_call | solution.py:481
  62.9 0.0 copy-start.3
  62.9 0.0 copy-start.4
  62.9 0.0 copy-done
  62.9 0.0 copy-done.1
  62.9 0.0 copy-done.2
  62.9 0.6 copy-done.3
  63.5 0.0 copy-done.4
  63.5 0.8 %convert_element_type.18 = f32[64,2048]{1,0:T(8,128)} convert(bf16[64,2048]{1,0:T(8,128)(2,1)S(1)} %get-tuple-element.42) | non-fusion elementwise | flops 131072 | bytes 786432 | tf_op jit(solution)/shard_map/convert_element_type | solution.py:543
  64.4 0.6 copy.12
  (1 shorter events, 0.0 us)
Async XLA Ops:
  0.6 62.3 %copy-start = (f32[90,2048]{1,0:T(8,128)S(1)}, f32[90,2048]{1,0:T(8,128)}, u32[]{:S(2)}) copy-start(f32[90,2048]{1,0:T(8,128)} %pts_hbm.1) | copy-start | bytes 2211844
  0.6 62.3 %copy-start.1 = (bf16[64,2048]{1,0:T(8,128)(2,1)S(1)}, bf16[64,2048]{1,0:T(8,128)(2,1)}, u32[]{:S(2)}) copy-start(bf16[64,2048]{1,0:T(8,128)(2,1)} %left_hbm.1) | copy-start | bytes 786436
  0.6 62.3 %copy-start.2 = (bf16[64,256]{1,0:T(8,128)(2,1)S(1)}, bf16[64,256]{1,0:T(8,128)(2,1)}, u32[]{:S(2)}) copy-start(bf16[64,256]{1,0:T(8,128)(2,1)} %right_hbm.1) | copy-start | bytes 98308
  62.9 0.7 %copy-start.3 = (s32[256]{0:T(256)S(1)}, s32[256]{0:T(256)}, u32[]{:S(2)}) copy-start(s32[256]{0:T(256)} %param.8) | copy-start | bytes 3076
  62.9 0.7 %copy-start.4 = (f32[90]{0:T(128)S(1)}, f32[90]{0:T(128)}, u32[]{:S(2)}) copy-start(f32[90]{0:T(128)} %param.9) | copy-start | bytes 1084
